TPU v7x, 128 devices: a whole 4x4x4 slice. The times are simulated.
128 devices in a mesh: group: 8 (over y, core), tp: 16 (over x, z).
Axes of the slice: x: 4, y: 4, z: 4, core: 2. Of those that a mesh axis runs over, the one named last changes fastest.
Arguments:
- residual: bfloat16 [768, 4096], P('group', 'tp'), may hold values from -18 to 18
- tree_qkv: bfloat16 [3, 768, 4096], P(None, 'group', 'tp'), may hold values from -12.5 to 12.5
- kv_pool: bfloat16 [2, 256, 128, 4096], P(None, 'group', None, 'tp'), may hold values from -12.5 to 12.5
- page_table: int32 [16, 28], replicated, may hold values from 0 to 31, as said below
- cache_len: int32 [16], replicated, may hold values from 1 to 3584, as said below
- tree_parent: int32 [16, 48], replicated, may hold values from 0 to 46, as said below
- accepted_nodes: int32 [16, 4], P('group'), may hold values from 0 to 47
- out_weight: bfloat16 [4096, 4096], P('tp'), may hold values from -0.125 to 0.125
- norm_gain: float32 [4096], P('tp'), may hold values from 0.5 to 1.5
- draft_weight: bfloat16 [3, 4096, 4096], P(None, None, 'tp'), may hold values from -0.09375 to 0.09375
- vocab_weight: bfloat16 [26624, 4096], P('tp'), may hold values from -1.75 to 1.75
- target_ids: int32 [4, 768], P(None, 'group'), may hold values from 0 to 26623
Outputs:
- log_probs: float32 [4, 768], P(None, 'group')
- accepted_kv: bfloat16 [2, 64, 4096], P(None, 'group', 'tp')
Inputs may be any that keep to these rules, and one draw needn't show every extreme that they name: `cache_len`: request 2 g is group g's short request and request 2 g + 1 its long one; a short request has at most 512 positions and some group's has exactly that many; a long request has 128 or more and some group's has exactly 3584. `page_table`: entries of request r of group g = r // 2 are slots of group g's pool, except the odd columns of a long request, which are slots of group g xor 1's pool. In each group's pool the short request's first 4 columns, its long request's even columns and the odd columns of group g xor 1's long request are distinct slots covering the pool; a short request's columns from 4 on repeat its first ones. `tree_parent`: node 0 is the root and its own parent; every other node's parent has a smaller index, and node 48 - 1's parent is node 46.
All inputs are finite; a program needn't handle non-finite values.
Results may differ from a plain program's by a relative error of at most 0.004.
Values may be sent and summed in bfloat16 or wider, within the bound.
A program may use at most 128 MiB of HBM per device.

v0:
```python
import math
import jax
import jax.numpy as jnp
from jax import lax
from jax.sharding import PartitionSpec as P

D = 4096
HEADS = 32
HD = 128
TREE = 48
SHORT_PAGES = 4
LONG_PAGES = 28
EPSILON = 1e-05


def from_partner(block, axis, apart):
    count = lax.axis_size(axis)
    route = []
    for low in range(count):
        high = low | 1 << apart
        if high != low and high < count:
            route += [(low, high), (high, low)]
    return lax.ppermute(block, axis, route)


def combined_all(array, axis, combine):
    everything = jax.tree.map(lambda part: lax.all_gather(part, axis), array)
    leading = jax.tree.map(lambda part: part[0], everything)

    def turn(k, so_far):
        return combine(so_far, jax.tree.map(lambda part: part[k], everything))

    return lax.fori_loop(1, lax.axis_size(axis), turn, leading)


def ancestry(parents):
    number = parents.shape[0]
    indices = jnp.arange(number, dtype=jnp.int32)
    linked = ((parents[:, None] == indices[None, :]) & (indices[:, None] > 0)).astype(jnp.float32)
    reached = jnp.minimum(jnp.eye(number, dtype=jnp.float32) + linked, 1.0)
    for sweep_index in range(max(1, number.bit_length())):
        reached = jnp.minimum(jnp.dot(reached, reached, precision=lax.Precision.HIGHEST), 1.0)
    depths = jnp.sum(reached, axis=1) - 1.0
    return (reached, depths)


def slope_values(first, number):
    ordinal = jnp.arange(number, dtype=jnp.float32) + jnp.asarray(first, jnp.float32) + 1.0
    return jnp.exp2(-8.0 * ordinal / HEADS)


def partial_attention(queries, key_rows, value_rows, allowed, query_pos, key_pos, slopes):
    scores = jnp.einsum("thd,lhd->htl", queries, key_rows, preferred_element_type=jnp.float32) * (
        1.0 / math.sqrt(HD)
    )
    scores = scores - slopes[:, None, None] * (query_pos[None, :, None] - key_pos[None, None, :])
    row_top = jnp.max(jnp.where(allowed[None], scores, -1e30), axis=2)
    weights = jnp.where(allowed[None], jnp.exp(scores - row_top[:, :, None]), 0.0)
    weight_sum = jnp.sum(weights, axis=2)
    weighted = jnp.einsum(
        "htl,lhd->thd", weights, value_rows.astype(jnp.float32), precision=lax.Precision.HIGHEST
    )
    return (row_top, weight_sum, weighted)


def join_parts(earlier, later):
    joined = jnp.maximum(earlier[0], later[0])
    factor_one = jnp.exp(earlier[0] - joined)
    factor_two = jnp.exp(later[0] - joined)
    weight_sum = earlier[1] * factor_one + later[1] * factor_two
    weighted = (
        earlier[2] * jnp.transpose(factor_one)[:, :, None]
        + later[2] * jnp.transpose(factor_two)[:, :, None]
    )
    return (joined, weight_sum, weighted)


def page_attention(gathered, columns, queries, query_pos, length, slopes, heads_dev):
    number = gathered.shape[1]
    page_rows = gathered.shape[2]
    flat_pages = gathered.reshape(2, number * page_rows, heads_dev, HD)
    key_pos = (
        (columns[:, None] * page_rows + jnp.arange(page_rows)[None, :])
        .reshape(-1)
        .astype(jnp.float32)
    )
    allowed = jnp.broadcast_to(key_pos[None, :] < length, (queries.shape[0], key_pos.shape[0]))
    return partial_attention(
        queries, flat_pages[0], flat_pages[1], allowed, query_pos, key_pos, slopes
    )


def merge_softmax(earlier, later):
    joined = jnp.maximum(earlier[0], later[0])
    return (
        joined,
        earlier[1] * jnp.exp(earlier[0] - joined) + later[1] * jnp.exp(later[0] - joined),
        earlier[2] + later[2],
    )


def shards(
    residual,
    tree_qkv,
    kv_pool,
    page_table,
    cache_len,
    tree_parent,
    accepted_nodes,
    out_weight,
    norm_gain,
    draft_weight,
    vocab_weight,
    target_ids,
):
    lane_count = lax.axis_size("tp")
    lane_index = lax.axis_index("tp")
    group_index = lax.axis_index("group")
    partner = jnp.bitwise_xor(group_index, 1)
    heads_dev = HEADS // lane_count
    width_dev = residual.shape[1]
    slopes = slope_values(lane_index * heads_dev, heads_dev)
    odd_columns = jnp.arange(1, LONG_PAGES, 2, dtype=jnp.int32)
    attn_rows = []
    for slot_index in range(2):
        request = group_index * 2 + slot_index
        tree_block = tree_qkv[:, slot_index * TREE : (slot_index + 1) * TREE].reshape(
            3, TREE, heads_dev, HD
        )
        reached, depths = ancestry(tree_parent[request])
        length = cache_len[request].astype(jnp.float32)
        query_pos = length + depths
        merged = partial_attention(
            tree_block[0], tree_block[1], tree_block[2], reached > 0.5, query_pos, query_pos, slopes
        )
        table_row = page_table[request]
        if slot_index == 0:
            own_columns = jnp.arange(SHORT_PAGES, dtype=jnp.int32)
            own_slots = table_row[:SHORT_PAGES]
        else:
            own_columns = jnp.arange(0, LONG_PAGES, 2, dtype=jnp.int32)
            own_slots = table_row[0::2]
        own_pages = jnp.take(kv_pool, own_slots, axis=1)
        merged = join_parts(
            merged,
            page_attention(
                own_pages, own_columns, tree_block[0], query_pos, length, slopes, heads_dev
            ),
        )
        if slot_index == 1:
            guest_req = partner * 2 + 1
            visitors = from_partner(tree_block[0], "group", 0)
            guest_len = cache_len[guest_req].astype(jnp.float32)
            guest_pos = guest_len + ancestry(tree_parent[guest_req])[1]
            held_pages = jnp.take(kv_pool, page_table[guest_req][1::2], axis=1)
            guest_part = page_attention(
                held_pages, odd_columns, visitors, guest_pos, guest_len, slopes, heads_dev
            )
            returned = from_partner((guest_part[0], guest_part[1], guest_part[2]), "group", 0)
            merged = join_parts(merged, returned)
        row_top, weight_sum, weighted = merged
        attn_rows.append(
            (weighted / jnp.transpose(weight_sum)[:, :, None])
            .reshape(TREE, width_dev)
            .astype(jnp.bfloat16)
        )
    attn = jnp.concatenate(attn_rows, 0)
    head_term = jnp.dot(attn, out_weight, preferred_element_type=jnp.float32)
    head_share = lax.psum_scatter(
        head_term.astype(jnp.bfloat16), "tp", scatter_dimension=1, tiled=True
    ).astype(jnp.float32)
    hidden = residual.astype(jnp.float32) + head_share
    row_sums, squares = lax.psum((jnp.sum(hidden, axis=1), jnp.sum(hidden * hidden, axis=1)), "tp")
    row_mean = (row_sums / D)[:, None]
    row_var = (squares / D)[:, None] - row_mean * row_mean
    normed = ((hidden - row_mean) * lax.rsqrt(row_var + EPSILON) * norm_gain).astype(jnp.bfloat16)
    normed_full = lax.all_gather(normed, "tp", axis=1, tiled=True)
    updates = jnp.einsum(
        "td,kdc->ktc", normed_full, draft_weight, preferred_element_type=jnp.float32
    )
    drafted = (normed.astype(jnp.float32)[None] + jax.nn.silu(updates)).astype(jnp.bfloat16)
    vocab_dev = vocab_weight.shape[0]
    base_logits = lax.dot_general(
        vocab_weight, normed_full, (((1,), (1,)), ((), ())), preferred_element_type=jnp.float32
    )
    draft_logits = jnp.einsum(
        "vc,ktc->vkt",
        vocab_weight,
        lax.all_gather(drafted, "tp", axis=2, tiled=True),
        preferred_element_type=jnp.float32,
    )
    logits = jnp.concatenate([base_logits[:, None, :], draft_logits], 1)
    local_top = jnp.max(logits, axis=0)
    local_total = jnp.sum(jnp.exp(logits - local_top[None]), axis=0)
    vocab_ids = lane_index * vocab_dev + jnp.arange(vocab_dev, dtype=jnp.int32)
    matches = vocab_ids[:, None, None] == target_ids[None]
    local_pick = jnp.sum(jnp.where(matches, logits, 0.0), axis=0)
    global_top, global_total, picked = combined_all(
        (local_top, local_total, local_pick), "tp", merge_softmax
    )
    log_probs = picked - (global_top + jnp.log(global_total))
    flat_index = (jnp.arange(2, dtype=jnp.int32)[:, None] * TREE + accepted_nodes).reshape(-1)
    accepted_kv = jnp.take(tree_qkv[1:3], flat_index, axis=1)
    return (log_probs, accepted_kv)


def solution(mesh):
    placed = (
        P("group", "tp"),
        P(None, "group", "tp"),
        P(None, "group", None, "tp"),
        P(),
        P(),
        P(),
        P("group", None),
        P("tp", None),
        P("tp"),
        P(None, None, "tp"),
        P("tp", None),
        P(None, "group"),
    )
    return jax.shard_map(
        shards,
        mesh=mesh,
        in_specs=placed,
        out_specs=(P(None, "group"), P(None, "group", "tp")),
        check_vma=False,
    )
```

profile of v0, /device:TPU:0, one launch (start us, length us, event | category | flops | bytes accessed | tf_op | source)
XLA Modules:
  0.0 353.4 jit_solution(13451830431486187444)
XLA Ops:
  7.2 1.0 fusion.128
  8.2 0.6 copy.49
  8.9 0.8 constant_dynamic-slice_fusion.4
  9.9 0.8 fusion.102
  11.9 1.4 fusion.129
  14.0 0.7 broadcast_compare_fusion.4
  14.7 0.7 broadcast_subtract_fusion.4
  15.4 2.8 gather_fusion
  18.4 0.8 squeeze.91
  19.1 0.6 squeeze.88
  19.7 0.6 multiply_exponential_fusion
  20.4 0.7 copy.38
  21.0 0.6 squeeze.89
  21.6 0.8 squeeze.92
  22.4 0.6 squeeze.90
  23.0 4.1 %gather_fusion.3 = bf16[14,2,128,256]{3,2,1,0:T(8,128)(2,1)} fusion(bf16[2,32,128,256]{3,2,1,0:T(8,128)(2,1)} %param.18, s32[1024]{0:T(1024)S(1)} %pad_clamp_fusion.1), kind=kCustom, calls=%fused_computation.1.clone | custom fusion | bytes 3670072 | tf_op jit(solution)/shard_map/jit(_take)/gather | solution.py:155
  27.2 1.7 select_bitcast_fusion
  28.9 1.1 fusion.126
  31.8 0.7 convert_bitcast_fusion
  32.4 0.7 broadcast_compare_fusion.2
  33.6 4.1 %gather_fusion.2 = bf16[14,2,128,256]{3,2,1,0:T(8,128)(2,1)} fusion(bf16[2,32,128,256]{3,2,1,0:T(8,128)(2,1)} %param.18, s32[1024]{0:T(1024)S(1)} %pad_clamp_fusion.2), kind=kCustom, calls=%fused_computation.clone | custom fusion | bytes 3670072 | tf_op jit(solution)/shard_map/jit(_take)/gather | solution.py:143
  37.7 1.7 select_bitcast_fusion.1
  39.4 1.4 fusion.125
  40.8 2.9 squeeze.97
  45.6 0.7 broadcast_compare_fusion.3
  46.2 0.7 broadcast_subtract_fusion.3
  47.6 1.4 copy.48
  48.9 0.6 squeeze.94
  49.6 1.7 select_reduce_fusion.2
  51.3 0.8 copy-done.2
  52.1 1.5 fusion.31
  53.6 0.8 select_reduce_fusion.4
  54.5 0.6 fusion.98
  55.1 1.3 select_reduce_fusion.3
  56.3 0.8 fusion.43
  57.2 0.9 select_reduce_fusion.5
  58.1 0.7 fusion.51
  58.9 1.3 fusion.22
  60.2 0.8 broadcast_subtract_fusion
  60.9 0.9 fusion.16
  61.9 1.0 fusion.24
  62.9 0.7 fusion.52
  63.7 2.9 squeeze.100
  66.6 1.1 squeeze.101
  67.7 2.2 squeeze.98
  70.0 1.8 select_reduce_fusion.1
  72.7 0.7 convolution_bitcast_fusion.2
  74.0 0.8 collective-permute-done.2
  74.8 0.7 fusion.66
  75.6 1.4 convolution_convert_fusion
  77.2 75.3 %reduce-scatter.2.cloned.1.call-done = bf16[96,256]{1,0:T(8,128)(2,1)} async-done(((bf16[96,4096]{1,0:T(8,128)(2,1)}), bf16[96,256]{1,0:T(8,128)(2,1)}) %reduce-scatter.2.cloned.1.call-update) | async-done | bytes 49168 | tf_op jit(solution)/shard_map/reduce_scatter | solution.py:169
  152.5 0.9 fusion.47
  153.4 38.1 %all-reduce = (f32[96]{0:T(128)S(1)}, f32[96]{0:T(128)S(1)}) all-reduce(f32[96]{0:T(128)S(1)} %get-tuple-element.191, f32[96]{0:T(128)S(1)} %get-tuple-element.190), channel_id=1, replica_groups=mesh['group'=8,'tp'=16] {'tp'}, use_global_device_ids=true, to_apply=%region_17.19 | all-reduce | flops 192 | bytes 1536 | tf_op jit(solution)/shard_map/psum | solution.py:173
  191.5 0.9 fusion.122
  192.4 21.9 %all_gather.24 = bf16[96,4096]{1,0:T(8,128)(2,1)S(1)} all-gather(bf16[96,256]{1,0:T(8,128)(2,1)S(1)} %get-tuple-element.211), channel_id=1, replica_groups=mesh['group'=8,'tp'=16] {'tp'}, dimensions={1}, use_global_device_ids=true | all-gather | bytes 835584 | tf_op jit(solution)/shard_map/all_gather | solution.py:177
  214.4 4.7 %add_convert_fusion = bf16[3,96,256]{2,1,0:T(8,128)(2,1)} fusion(bf16[3,4096,256]{2,1,0:T(8,128)(2,1)} %param.25, bf16[96,4096]{1,0:T(8,128)(2,1)S(1)} %all_gather.24, f32[96,256]{1,0:T(8,128)S(1)} %get-tuple-element.210), kind=kOutput, calls=%fused_computation.86 | convolution fusion | flops 604422144 | bytes 7323648 | tf_op jit(solution)/shard_map/td,kdc->ktc/dot_general | solution.py:178
  220.7 9.1 %convolution_bitcast_fusion = f32[1664,1,96]{0,2,1:T(8,128)S(1)} fusion(bf16[96,4096]{1,0:T(8,128)(2,1)S(1)} %all_gather.24, bf16[1664,4096]{1,0:T(8,128)(2,1)} %param.26), kind=kOutput, calls=%fused_computation.23 | convolution fusion | flops 1308622848 | bytes 15056896 | tf_op jit(solution)/shard_map/dot_general | solution.py:183
  229.8 38.5 %all-gather.8.cloned.1.call-done = bf16[3,96,4096]{2,1,0:T(8,128)(2,1)} async-done(((bf16[3,96,256]{2,1,0:T(8,128)(2,1)}), bf16[3,96,4096]{2,1,0:T(8,128)(2,1)}) %all-gather.8.cloned.1.call-update) | async-done | bytes 2359312 | tf_op jit(solution)/shard_map/all_gather | solution.py:189
  268.3 9.1 %fusion.4 = f32[1664,3,96]{0,2,1:T(8,128)S(1)} fusion(bf16[3,96,4096]{2,1,0:T(8,128)(2,1)} %all-gather.8.cloned.1.call-done, bf16[1664,4096]{1,0:T(8,128)(2,1)} %param.26), kind=kOutput, calls=%fused_computation.13 | convolution fusion | flops 3925868544 | bytes 17907712 | tf_op jit(solution)/shard_map/vc,ktc->vkt/dot_general | solution.py:186
  278.1 0.8 select_reduce_fusion
  278.9 22.6 %all-gather.5 = f32[16,4,96]{2,1,0:T(4,128)S(1)} all-gather(f32[1,4,96]{2,1,0:T(4,128)S(1)} %bitcast.234), channel_id=4, replica_groups=mesh['group'=8,'tp'=16] {'tp'}, dimensions={0}, use_global_device_ids=true | all-gather | bytes 26112 | tf_op jit(solution)/shard_map/all_gather | solution.py:27
  301.6 21.1 %all-gather.4 = f32[16,4,96]{2,1,0:T(4,128)S(1)} all-gather(f32[1,4,96]{2,1,0:T(4,128)S(1)} %bitcast.233), channel_id=3, replica_groups=mesh['group'=8,'tp'=16] {'tp'}, dimensions={0}, use_global_device_ids=true | all-gather | bytes 26112 | tf_op jit(solution)/shard_map/all_gather | solution.py:27
  322.7 22.6 %all-gather.3 = f32[16,4,96]{2,1,0:T(4,128)S(1)} all-gather(f32[1,4,96]{2,1,0:T(4,128)S(1)} %bitcast.232), channel_id=2, replica_groups=mesh['group'=8,'tp'=16] {'tp'}, dimensions={0}, use_global_device_ids=true | all-gather | bytes 26112 | tf_op jit(solution)/shard_map/all_gather | solution.py:27
  345.3 0.7 while.19
  (134 shorter events, 10.3 us)
Async XLA Ops:
  7.2 68.4 %copy-start = (bf16[256,4096]{1,0:T(8,128)(2,1)S(1)}, bf16[256,4096]{1,0:T(8,128)(2,1)}, u32[]{:S(2)}) copy-start(bf16[256,4096]{1,0:T(8,128)(2,1)} %param.23) | copy-start | bytes 6291460
  7.2 145.3 %reduce-scatter.2.cloned.1.call-start = ((), (), s32[]{:S(2)}) async-start(), calls=%async_computation.1 | async-start | bytes 835584 | tf_op jit(solution)/shard_map/reduce_scatter | solution.py:169
  8.8 61.1 %collective-permute-start = (bf16[48,2,128]{2,0,1:T(8,128)(2,1)}, bf16[48,2,128]{2,0,1:T(8,128)(2,1)}, u32[]{:S(2)}, u32[]{:S(2)}) collective-permute-start(bf16[48,2,128]{2,0,1:T(8,128)(2,1)} %copy.49), channel_id=1, source_target_pairs={{0,16},{16,0},{32,48},{48,32},{64,80},{80,64},{96,112},{112,96},{1... | collective-permute-start | bytes 73736 | tf_op jit(solution)/shard_map/ppermute | solution.py:23
  49.6 4.0 %copy-start.5 = (pred[48,48]{0,1:T(8,128)(4,1)S(1)}, pred[48,48]{0,1:T(8,128)(4,1)}, u32[]{:S(2)}) copy-start(pred[48,48]{0,1:T(8,128)(4,1)} %copy.48) | copy-start | bytes 6916
  49.6 4.0 %copy-start.6 = (f32[48,48]{0,1:T(8,128)S(1)}, f32[48,48]{0,1:T(8,128)}, u32[]{:S(2)}) copy-start(f32[48,48]{0,1:T(8,128)} %broadcast_subtract_fusion.3) | copy-start | bytes 27652
  49.6 4.0 %copy-start.7 = (bf16[48,2,128]{2,1,0:T(2,128)(2,1)S(1)}, bf16[48,2,128]{2,1,0:T(2,128)(2,1)}, u32[]{:S(2)}) copy-start(bf16[48,2,128]{2,1,0:T(2,128)(2,1)} %squeeze.94) | copy-start | bytes 73732
  51.3 0.9 copy-start.2
  51.3 3.8 %copy-start.10 = (f32[2,48]{1,0:T(2,128)}, f32[2,48]{1,0:T(2,128)S(1)}, u32[]{:S(2)}) copy-start(f32[2,48]{1,0:T(2,128)S(1)} %get-tuple-element.250) | copy-start | bytes 1156
  54.4 4.4 %copy-start.8 = (f32[2,48]{1,0:T(2,128)}, f32[2,48]{1,0:T(2,128)S(1)}, u32[]{:S(2)}) copy-start(f32[2,48]{1,0:T(2,128)S(1)} %get-tuple-element.248) | copy-start | bytes 1156
  63.6 6.3 %copy-start.12 = (pred[1792]{0:T(1024)(128)(4,1)S(1)}, pred[1792]{0:T(1024)(128)(4,1)}, u32[]{:S(2)}) copy-start(pred[1792]{0:T(1024)(128)(4,1)} %broadcast_compare_fusion.2) | copy-start | bytes 5380
  63.6 6.3 %copy-start.19 = (f32[2]{0:T(128)S(1)}, f32[2]{0:T(128)}, u32[]{:S(2)}) copy-start(f32[2]{0:T(128)} %multiply_exponential_fusion) | copy-start | bytes 28
  69.9 2.8 copy-start.1
  69.9 4.1 %copy-start.9 = (f32[2,48]{1,0:T(2,128)S(1)}, f32[2,48]{1,0:T(2,128)}, u32[]{:S(2)}) copy-start(f32[2,48]{1,0:T(2,128)} %copy-done.8) | copy-start | bytes 1156
  69.9 4.1 %copy-start.11 = (f32[2,48]{1,0:T(2,128)S(1)}, f32[2,48]{1,0:T(2,128)}, u32[]{:S(2)}) copy-start(f32[2,48]{1,0:T(2,128)} %copy-done.10) | copy-start | bytes 1156
  69.9 4.1 %copy-start.14 = (f32[2,48]{1,0:T(2,128)S(1)}, f32[2,48]{1,0:T(2,128)}, u32[]{:S(2)}) copy-start(f32[2,48]{1,0:T(2,128)} %fusion.31) | copy-start | bytes 1156
  69.9 4.9 %copy-start.3 = (f32[2,48,1792]{2,1,0:T(8,128)S(1)}, f32[2,48,1792]{2,1,0:T(8,128)}, u32[]{:S(2)}) copy-start(f32[2,48,1792]{2,1,0:T(8,128)} %copy-done.2) | copy-start | bytes 2064388
  69.9 4.9 %copy-start.13 = (pred[1792]{0:T(1024)(128)(4,1)S(1)}, pred[1792]{0:T(1024)(128)(4,1)}, u32[]{:S(2)}) copy-start(pred[1792]{0:T(1024)(128)(4,1)} %broadcast_compare_fusion.3) | copy-start | bytes 5380
  69.9 4.9 %copy-start.18 = (f32[48,2]{0,1:T(2,128)S(1)}, f32[48,2]{0,1:T(2,128)}, u32[]{:S(2)}) copy-start(f32[48,2]{0,1:T(2,128)} %get-tuple-element.237) | copy-start | bytes 1156
  71.8 2.2 collective-permute-start.1
  72.6 1.3 collective-permute-start.3
  73.4 1.4 collective-permute-start.2
  75.6 76.9 %copy-start.4 = (bf16[96,256]{1,0:T(8,128)(2,1)S(1)}, bf16[96,256]{1,0:T(8,128)(2,1)}, u32[]{:S(2)}) copy-start(bf16[96,256]{1,0:T(8,128)(2,1)} %param.16) | copy-start | bytes 147460
  75.6 116.0 %copy-start.16 = (f32[256]{0:T(256)S(1)}, f32[256]{0:T(256)}, u32[]{:S(2)}) copy-start(f32[256]{0:T(256)} %param.24) | copy-start | bytes 3076
  77.0 191.3 %all-gather.8.cloned.1.call-start = ((), (), s32[]{:S(2)}) async-start(), calls=%async_computation.2 | async-start | bytes 2506752 | tf_op jit(solution)/shard_map/all_gather | solution.py:189
  214.4 4.7 %copy-start.17 = (s32[2,4]{1,0:T(2,128)S(1)}, s32[2,4]{1,0:T(2,128)}, u32[]{:S(2)}) copy-start(s32[2,4]{1,0:T(2,128)} %param.22) | copy-start | bytes 100
  214.4 5.0 %slice-start = ((bf16[3,96,256]{2,1,0:T(8,128)(2,1)}), bf16[2,96,256]{2,1,0:T(8,128)(2,1)S(1)}, s32[]{:S(2)}) async-start(bf16[3,96,256]{2,1,0:T(8,128)(2,1)} %param.17), calls=%async_computation.3 | async-start | bytes 196608 | tf_op jit(solution)/shard_map/slice | solution.py:203
  277.4 0.7 copy-start.15
Sparse Core Ops, SparseCore 0:
  77.1 75.3 reduce-scatter.1
  219.2 49.0 all-gather.7
where the time goes:
time: 355 us; the launch traced here: 353 us
  blocking collectives  126 us (35%)
  waiting for transfers between devices  115 us (32%)
  matrix products  38.7 us (11%)
  local copies, waits for them, and re-layouts  36.3 us (10%)
  other arithmetic  19.1 us (5%)
  between operations  16.6 us (5%)
    reduce_scatter x1, waiting for transfers between devices, shards(): lax.psum_scatter(head_term.astype(jnp.bfloat16), 'tp', scatter_dimension=...  75.3 us
    all_gather x3, blocking collectives, combined_all(): everything = jax.tree.map(lambda part: lax.all_gather(part, axis), array)  66.4 us
    all_gather x1, waiting for transfers between devices, shards(): lax.all_gather(drafted, 'tp', axis=2, tiled=True)  38.5 us
    psum x1, blocking collectives, shards(): lax.psum((jnp.sum(hidden, axis=1), jnp.sum(hidden * hidden, axis=1)), 'tp')  38.1 us
    all_gather x1, blocking collectives, shards(): normed_full = lax.all_gather(normed, 'tp', axis=1, tiled=True)  21.9 us
    dot_general x1, matrix products, shards(): jnp.einsum('vc,ktc->vkt', vocab_weight, lax.all_gather(drafted, 'tp', axi...  9.1 us
    dot_general x1, matrix products, shards(): lax.dot_general(vocab_weight, normed_full, (((1,), (1,)), ((), ())), pref...  9.1 us
  transfers between devices with their start and end apart: 6, of which 3 were waited for; matrix products, arithmetic and copies ran while one was open for 20% of the time, Pallas kernels for 0%

commit v1 on v0

--- a/solution.py
+++ b/solution.py
@@ -174,7 +174,34 @@
     row_mean = (row_sums / D)[:, None]
     row_var = (squares / D)[:, None] - row_mean * row_mean
     normed = ((hidden - row_mean) * lax.rsqrt(row_var + EPSILON) * norm_gain).astype(jnp.bfloat16)
-    normed_full = lax.all_gather(normed, "tp", axis=1, tiled=True)
+
+    def show_shapes(axis_name, xs):
+        before = lax.psum(1, axis_name=axis_name)
+        state_next = lax.axis_index(axis_name)
+        all_rows, reply, new = (before, state_next, xs.shape[1])
+        res = tmp = xs
+        even = lax.dynamic_update_slice_in_dim(
+            jnp.zeros([ix * all_rows if b == 1 else ix for b, ix in enumerate(xs.shape)], xs.dtype),
+            xs,
+            reply * new,
+            axis=1,
+        )
+        for at in range(1, all_rows // 2 + 1):
+            res = lax.ppermute(
+                res,
+                axis_name=axis_name,
+                perm=list(map(lambda b: (b, (b + 1) % all_rows), range(all_rows))),
+            )
+            even = lax.dynamic_update_slice_in_dim(even, res, (reply - at) % all_rows * new, axis=1)
+            if 2 * at < all_rows:
+                heard = list(map(lambda b: (b, (b - 1) % all_rows), range(all_rows)))
+                tmp = lax.ppermute(tmp, axis_name=axis_name, perm=heard)
+                even = lax.dynamic_update_slice_in_dim(
+                    even, tmp, (reply + at) % all_rows * new, axis=1
+                )
+        return even
+
+    normed_full = show_shapes("tp", normed)
     updates = jnp.einsum(
         "td,kdc->ktc", normed_full, draft_weight, preferred_element_type=jnp.float32
     )

time: 355 us -> 389 us (1.096)
  starting transfers between devices: 1.46 us -> 40 us
  blocking collectives: 126 us -> 104 us
  waiting for transfers between devices: 115 us -> 131 us
    ppermute x0 -> x15, starting transfers between devices: none -> 38.5 us  [the longest x7 38.4 us: show_shapes(): tmp = lax.ppermute(tmp, axis_name=axis_name, perm=heard)]
    all_gather x1 -> x0, blocking collectives: 21.9 us -> none  [shards(): normed_full = lax.all_gather(normed, 'tp', axis=1, tiled=True)]
    ppermute x0 -> x15, waiting for transfers between devices: none -> 20.8 us  [the longest x8 20.8 us: show_shapes(): lax.ppermute(res, axis_name=axis_name, perm=list(map(lambda b: (b, (b + 1...]
    all_gather x1, waiting for transfers between devices: 38.5 us -> 34.5 us  [shards(): lax.all_gather(drafted, 'tp', axis=2, tiled=True)]
  transfers between devices with their start and end apart: 6 -> 21, of which waited for: 3 -> 11; matrix products, arithmetic and copies ran while one was open for 20% -> 18% of each run, Pallas kernels for 0% -> 0%
where the time goes in v1:
time: 389 us; the launch traced here: 387 us
  waiting for transfers between devices  131 us (34%)
  blocking collectives  104 us (27%)
  starting transfers between devices  40 us (10%)
  matrix products  38.7 us (10%)
  local copies, waits for them, and re-layouts  36.6 us (9%)
  other arithmetic  19.2 us (5%)
  between operations  17 us (4%)
    reduce_scatter x1, waiting for transfers between devices, shards(): lax.psum_scatter(head_term.astype(jnp.bfloat16), 'tp', scatter_dimension=...  74.9 us
    all_gather x3, blocking collectives, combined_all(): everything = jax.tree.map(lambda part: lax.all_gather(part, axis), array)  66.4 us
    ppermute x7, starting transfers between devices, show_shapes(): tmp = lax.ppermute(tmp, axis_name=axis_name, perm=heard)  38.4 us
    psum x1, blocking collectives, shards(): lax.psum((jnp.sum(hidden, axis=1), jnp.sum(hidden * hidden, axis=1)), 'tp')  38.1 us
    all_gather x1, waiting for transfers between devices, shards(): lax.all_gather(drafted, 'tp', axis=2, tiled=True)  34.5 us
    ppermute x8, waiting for transfers between devices, show_shapes(): lax.ppermute(res, axis_name=axis_name, perm=list(map(lambda b: (b, (b + 1...  20.8 us
    dot_general x1, matrix products, shards(): lax.dot_general(vocab_weight, normed_full, (((1,), (1,)), ((), ())), pref...  9.17 us
    dot_general x1, matrix products, shards(): jnp.einsum('vc,ktc->vkt', vocab_weight, lax.all_gather(drafted, 'tp', axi...  9.1 us
  transfers between devices with their start and end apart: 21, of which 11 were waited for; matrix products, arithmetic and copies ran while one was open for 18% of the time, Pallas kernels for 0%

profile of v1, /device:TPU:0, one launch (start us, length us, event | category | flops | bytes accessed | tf_op | source)
XLA Modules:
  0.0 387.4 jit_solution(4651042847714952508)
XLA Ops:
  7.2 1.0 fusion.128
  8.8 0.8 constant_dynamic-slice_fusion.4
  9.9 0.8 fusion.104
  11.9 1.4 fusion.129
  15.5 2.8 gather_fusion
  18.4 0.7 squeeze.91
  20.4 0.7 copy.38
  21.7 0.8 squeeze.92
  23.1 4.1 %gather_fusion.3 = bf16[14,2,128,256]{3,2,1,0:T(8,128)(2,1)} fusion(bf16[2,32,128,256]{3,2,1,0:T(8,128)(2,1)} %param.18, s32[1024]{0:T(1024)S(1)} %pad_clamp_fusion.1), kind=kCustom, calls=%fused_computation.1.clone | custom fusion | bytes 3670072 | tf_op jit(solution)/shard_map/jit(_take)/gather | solution.py:155
  27.2 1.7 select_bitcast_fusion
  28.9 1.1 fusion.126
  33.7 4.1 %gather_fusion.2 = bf16[14,2,128,256]{3,2,1,0:T(8,128)(2,1)} fusion(bf16[2,32,128,256]{3,2,1,0:T(8,128)(2,1)} %param.18, s32[1024]{0:T(1024)S(1)} %pad_clamp_fusion.2), kind=kCustom, calls=%fused_computation.clone | custom fusion | bytes 3670072 | tf_op jit(solution)/shard_map/jit(_take)/gather | solution.py:143
  37.8 1.7 select_bitcast_fusion.1
  39.6 1.4 fusion.125
  40.9 2.9 squeeze.97
  47.8 1.4 copy.48
  49.8 1.7 select_reduce_fusion.2
  51.5 0.8 copy-done.2
  52.4 1.5 fusion.31
  53.9 0.8 select_reduce_fusion.4
  55.3 1.3 select_reduce_fusion.3
  56.6 0.9 fusion.43
  57.4 0.9 select_reduce_fusion.5
  58.3 0.7 fusion.51
  59.1 1.3 fusion.22
  60.4 0.8 broadcast_subtract_fusion
  61.2 0.9 fusion.16
  62.1 1.0 fusion.24
  63.1 0.7 fusion.52
  63.9 2.9 squeeze.100
  66.8 1.1 squeeze.101
  67.9 2.2 squeeze.98
  70.2 1.8 select_reduce_fusion.1
  72.9 0.7 convolution_bitcast_fusion.2
  74.2 0.8 collective-permute-done.2
  75.1 0.7 fusion.66
  75.8 1.4 convolution_convert_fusion
  77.7 74.9 %reduce-scatter.2.cloned.1.call-done = bf16[96,256]{1,0:T(8,128)(2,1)} async-done(((bf16[96,4096]{1,0:T(8,128)(2,1)}), bf16[96,256]{1,0:T(8,128)(2,1)}) %reduce-scatter.2.cloned.1.call-update) | async-done | bytes 49168 | tf_op jit(solution)/shard_map/reduce_scatter | solution.py:169
  152.6 0.9 fusion.47
  153.6 38.1 %all-reduce = (f32[96]{0:T(128)S(1)}, f32[96]{0:T(128)S(1)}) all-reduce(f32[96]{0:T(128)S(1)} %get-tuple-element.191, f32[96]{0:T(128)S(1)} %get-tuple-element.190), channel_id=1, replica_groups=mesh['group'=8,'tp'=16] {'tp'}, use_global_device_ids=true, to_apply=%region_17.19 | all-reduce | flops 192 | bytes 1536 | tf_op jit(solution)/shard_map/psum | solution.py:173
  191.7 0.9 fusion.122
  192.7 5.3 %collective-permute-start.5 = (bf16[96,256]{1,0:T(8,128)(2,1)S(1)}, bf16[96,256]{1,0:T(8,128)(2,1)S(1)}, u32[]{:S(2)}, u32[]{:S(2)}) collective-permute-start(bf16[96,256]{1,0:T(8,128)(2,1)S(1)} %get-tuple-element.211), channel_id=1, source_target_pairs={{0,15},{1,0},{2,1},{3,2},{4,3},{5,4},{6,5},{7,6},{8,7},{9,8},{10,9... | collective-permute-start | bytes 147464 | tf_op jit(solution)/shard_map/ppermute | solution.py:198
  198.1 2.0 collective-permute-done.4
  200.1 5.3 %collective-permute-start.7 = (bf16[96,256]{1,0:T(8,128)(2,1)S(1)}, bf16[96,256]{1,0:T(8,128)(2,1)S(1)}, u32[]{:S(2)}, u32[]{:S(2)}) collective-permute-start(bf16[96,256]{1,0:T(8,128)(2,1)S(1)} %collective-permute-done.5), channel_id=1, source_target_pairs={{0,15},{1,0},{2,1},{3,2},{4,3},{5,4},{6,5},{7,6},{8,7},{9,8},{10,9... | collective-permute-start | bytes 147464 | tf_op jit(solution)/shard_map/ppermute | solution.py:198
  205.4 2.0 collective-permute-done.6
  207.5 5.3 %collective-permute-start.9 = (bf16[96,256]{1,0:T(8,128)(2,1)S(1)}, bf16[96,256]{1,0:T(8,128)(2,1)S(1)}, u32[]{:S(2)}, u32[]{:S(2)}) collective-permute-start(bf16[96,256]{1,0:T(8,128)(2,1)S(1)} %collective-permute-done.7), channel_id=1, source_target_pairs={{0,15},{1,0},{2,1},{3,2},{4,3},{5,4},{6,5},{7,6},{8,7},{9,8},{10,9... | collective-permute-start | bytes 147464 | tf_op jit(solution)/shard_map/ppermute | solution.py:198
  212.8 2.3 collective-permute-done.8
  215.2 5.6 %collective-permute-start.11 = (bf16[96,256]{1,0:T(8,128)(2,1)S(1)}, bf16[96,256]{1,0:T(8,128)(2,1)S(1)}, u32[]{:S(2)}, u32[]{:S(2)}) collective-permute-start(bf16[96,256]{1,0:T(8,128)(2,1)S(1)} %collective-permute-done.9), channel_id=1, source_target_pairs={{0,15},{1,0},{2,1},{3,2},{4,3},{5,4},{6,5},{7,6},{8,7},{9,8},{10,9... | collective-permute-start | bytes 147464 | tf_op jit(solution)/shard_map/ppermute | solution.py:198
  220.8 1.8 collective-permute-done.10
  222.6 5.6 %collective-permute-start.13 = (bf16[96,256]{1,0:T(8,128)(2,1)S(1)}, bf16[96,256]{1,0:T(8,128)(2,1)S(1)}, u32[]{:S(2)}, u32[]{:S(2)}) collective-permute-start(bf16[96,256]{1,0:T(8,128)(2,1)S(1)} %collective-permute-done.11), channel_id=1, source_target_pairs={{0,15},{1,0},{2,1},{3,2},{4,3},{5,4},{6,5},{7,6},{8,7},{9,8},{10,9... | collective-permute-start | bytes 147464 | tf_op jit(solution)/shard_map/ppermute | solution.py:198
  228.2 1.8 collective-permute-done.12
  230.0 5.6 %collective-permute-start.15 = (bf16[96,256]{1,0:T(8,128)(2,1)S(1)}, bf16[96,256]{1,0:T(8,128)(2,1)S(1)}, u32[]{:S(2)}, u32[]{:S(2)}) collective-permute-start(bf16[96,256]{1,0:T(8,128)(2,1)S(1)} %collective-permute-done.13), channel_id=1, source_target_pairs={{0,15},{1,0},{2,1},{3,2},{4,3},{5,4},{6,5},{7,6},{8,7},{9,8},{10,9... | collective-permute-start | bytes 147464 | tf_op jit(solution)/shard_map/ppermute | solution.py:198
  235.6 1.8 collective-permute-done.14
  237.4 5.6 %collective-permute-start.17 = (bf16[96,256]{1,0:T(8,128)(2,1)S(1)}, bf16[96,256]{1,0:T(8,128)(2,1)S(1)}, u32[]{:S(2)}, u32[]{:S(2)}) collective-permute-start(bf16[96,256]{1,0:T(8,128)(2,1)S(1)} %collective-permute-done.15), channel_id=1, source_target_pairs={{0,15},{1,0},{2,1},{3,2},{4,3},{5,4},{6,5},{7,6},{8,7},{9,8},{10,9... | collective-permute-start | bytes 147464 | tf_op jit(solution)/shard_map/ppermute | solution.py:198
  243.0 1.8 collective-permute-done.16
  244.8 7.4 %collective-permute-done.18 = bf16[96,256]{1,0:T(8,128)(2,1)S(1)} collective-permute-done((bf16[96,256]{1,0:T(8,128)(2,1)S(1)}, bf16[96,256]{1,0:T(8,128)(2,1)S(1)}, u32[]{:S(2)}, u32[]{:S(2)}) %collective-permute-start.18) | collective-permute-done | bytes 49184 | tf_op jit(solution)/shard_map/ppermute | solution.py:190
  252.2 4.7 %add_convert_fusion = bf16[3,96,256]{2,1,0:T(8,128)(2,1)} fusion(bf16[3,4096,256]{2,1,0:T(8,128)(2,1)} %param.25, bf16[96,4096]{1,0:T(8,128)(2,1)S(1)} %constant_dynamic-update-slice_fusion, f32[96,256]{1,0:T(8,128)S(1)} %get-tuple-element.210), kind=kOutput, calls=%fused_computation.86 | convolution fusion | flops 604422144 | bytes 7323648 | tf_op jit(solution)/shard_map/td,kdc->ktc/dot_general | solution.py:205
  258.6 9.2 %convolution_bitcast_fusion = f32[1664,1,96]{0,2,1:T(8,128)S(1)} fusion(bf16[96,4096]{1,0:T(8,128)(2,1)S(1)} %constant_dynamic-update-slice_fusion, bf16[1664,4096]{1,0:T(8,128)(2,1)} %param.26), kind=kOutput, calls=%fused_computation.23 | convolution fusion | flops 1308622848 | bytes 15056896 | tf_op jit(solution)/shard_map/dot_general | solution.py:210
  267.8 34.5 %all-gather.8.cloned.1.call-done = bf16[3,96,4096]{2,1,0:T(8,128)(2,1)} async-done(((bf16[3,96,256]{2,1,0:T(8,128)(2,1)}), bf16[3,96,4096]{2,1,0:T(8,128)(2,1)}) %all-gather.8.cloned.1.call-update) | async-done | bytes 2359312 | tf_op jit(solution)/shard_map/all_gather | solution.py:216
  302.3 9.1 %fusion.4 = f32[1664,3,96]{0,2,1:T(8,128)S(1)} fusion(bf16[3,96,4096]{2,1,0:T(8,128)(2,1)} %all-gather.8.cloned.1.call-done, bf16[1664,4096]{1,0:T(8,128)(2,1)} %param.26), kind=kOutput, calls=%fused_computation.13 | convolution fusion | flops 3925868544 | bytes 17907712 | tf_op jit(solution)/shard_map/vc,ktc->vkt/dot_general | solution.py:213
  312.1 0.8 select_reduce_fusion
  312.9 22.6 %all-gather.5 = f32[16,4,96]{2,1,0:T(4,128)S(1)} all-gather(f32[1,4,96]{2,1,0:T(4,128)S(1)} %bitcast.234), channel_id=4, replica_groups=mesh['group'=8,'tp'=16] {'tp'}, dimensions={0}, use_global_device_ids=true | all-gather | bytes 26112 | tf_op jit(solution)/shard_map/all_gather | solution.py:27
  335.5 21.1 %all-gather.4 = f32[16,4,96]{2,1,0:T(4,128)S(1)} all-gather(f32[1,4,96]{2,1,0:T(4,128)S(1)} %bitcast.233), channel_id=3, replica_groups=mesh['group'=8,'tp'=16] {'tp'}, dimensions={0}, use_global_device_ids=true | all-gather | bytes 26112 | tf_op jit(solution)/shard_map/all_gather | solution.py:27
  356.7 22.6 %all-gather.3 = f32[16,4,96]{2,1,0:T(4,128)S(1)} all-gather(f32[1,4,96]{2,1,0:T(4,128)S(1)} %bitcast.232), channel_id=2, replica_groups=mesh['group'=8,'tp'=16] {'tp'}, dimensions={0}, use_global_device_ids=true | all-gather | bytes 26112 | tf_op jit(solution)/shard_map/all_gather | solution.py:27
  (180 shorter events, 19.6 us)
Async XLA Ops:
  7.2 68.6 %copy-start = (bf16[256,4096]{1,0:T(8,128)(2,1)S(1)}, bf16[256,4096]{1,0:T(8,128)(2,1)}, u32[]{:S(2)}) copy-start(bf16[256,4096]{1,0:T(8,128)(2,1)} %param.23) | copy-start | bytes 6291460
  7.2 145.5 %reduce-scatter.2.cloned.1.call-start = ((), (), s32[]{:S(2)}) async-start(), calls=%async_computation.1 | async-start | bytes 835584 | tf_op jit(solution)/shard_map/reduce_scatter | solution.py:169
  8.8 61.3 %collective-permute-start = (bf16[48,2,128]{2,0,1:T(8,128)(2,1)}, bf16[48,2,128]{2,0,1:T(8,128)(2,1)}, u32[]{:S(2)}, u32[]{:S(2)}) collective-permute-start(bf16[48,2,128]{2,0,1:T(8,128)(2,1)} %copy.49), channel_id=1, source_target_pairs={{0,16},{16,0},{32,48},{48,32},{64,80},{80,64},{96,112},{112,96},{1... | collective-permute-start | bytes 73736 | tf_op jit(solution)/shard_map/ppermute | solution.py:23
  49.8 4.1 %copy-start.5 = (pred[48,48]{0,1:T(8,128)(4,1)S(1)}, pred[48,48]{0,1:T(8,128)(4,1)}, u32[]{:S(2)}) copy-start(pred[48,48]{0,1:T(8,128)(4,1)} %copy.48) | copy-start | bytes 6916
  49.8 4.1 %copy-start.6 = (f32[48,48]{0,1:T(8,128)S(1)}, f32[48,48]{0,1:T(8,128)}, u32[]{:S(2)}) copy-start(f32[48,48]{0,1:T(8,128)} %broadcast_subtract_fusion.3) | copy-start | bytes 27652
  49.8 4.1 %copy-start.7 = (bf16[48,2,128]{2,1,0:T(2,128)(2,1)S(1)}, bf16[48,2,128]{2,1,0:T(2,128)(2,1)}, u32[]{:S(2)}) copy-start(bf16[48,2,128]{2,1,0:T(2,128)(2,1)} %squeeze.94) | copy-start | bytes 73732
  51.5 0.9 copy-start.2
  51.5 3.8 copy-start.10
  54.7 4.4 %copy-start.8 = (f32[2,48]{1,0:T(2,128)}, f32[2,48]{1,0:T(2,128)S(1)}, u32[]{:S(2)}) copy-start(f32[2,48]{1,0:T(2,128)S(1)} %get-tuple-element.248) | copy-start | bytes 1156
  63.8 6.3 %copy-start.12 = (pred[1792]{0:T(1024)(128)(4,1)S(1)}, pred[1792]{0:T(1024)(128)(4,1)}, u32[]{:S(2)}) copy-start(pred[1792]{0:T(1024)(128)(4,1)} %broadcast_compare_fusion.2) | copy-start | bytes 5380
  63.9 6.3 %copy-start.19 = (f32[2]{0:T(128)S(1)}, f32[2]{0:T(128)}, u32[]{:S(2)}) copy-start(f32[2]{0:T(128)} %multiply_exponential_fusion) | copy-start | bytes 28
  70.1 2.8 copy-start.1
  70.1 4.1 %copy-start.9 = (f32[2,48]{1,0:T(2,128)S(1)}, f32[2,48]{1,0:T(2,128)}, u32[]{:S(2)}) copy-start(f32[2,48]{1,0:T(2,128)} %copy-done.8) | copy-start | bytes 1156
  70.1 4.1 %copy-start.11 = (f32[2,48]{1,0:T(2,128)S(1)}, f32[2,48]{1,0:T(2,128)}, u32[]{:S(2)}) copy-start(f32[2,48]{1,0:T(2,128)} %copy-done.10) | copy-start | bytes 1156
  70.1 4.1 %copy-start.14 = (f32[2,48]{1,0:T(2,128)S(1)}, f32[2,48]{1,0:T(2,128)}, u32[]{:S(2)}) copy-start(f32[2,48]{1,0:T(2,128)} %fusion.31) | copy-start | bytes 1156
  70.1 4.9 %copy-start.3 = (f32[2,48,1792]{2,1,0:T(8,128)S(1)}, f32[2,48,1792]{2,1,0:T(8,128)}, u32[]{:S(2)}) copy-start(f32[2,48,1792]{2,1,0:T(8,128)} %copy-done.2) | copy-start | bytes 2064388
  70.1 4.9 %copy-start.13 = (pred[1792]{0:T(1024)(128)(4,1)S(1)}, pred[1792]{0:T(1024)(128)(4,1)}, u32[]{:S(2)}) copy-start(pred[1792]{0:T(1024)(128)(4,1)} %broadcast_compare_fusion.3) | copy-start | bytes 5380
  70.2 4.9 %copy-start.18 = (f32[48,2]{0,1:T(2,128)S(1)}, f32[48,2]{0,1:T(2,128)}, u32[]{:S(2)}) copy-start(f32[48,2]{0,1:T(2,128)} %get-tuple-element.237) | copy-start | bytes 1156
  72.0 2.2 collective-permute-start.1
  72.8 1.3 collective-permute-start.3
  73.6 1.4 collective-permute-start.2
  75.8 76.9 %copy-start.4 = (bf16[96,256]{1,0:T(8,128)(2,1)S(1)}, bf16[96,256]{1,0:T(8,128)(2,1)}, u32[]{:S(2)}) copy-start(bf16[96,256]{1,0:T(8,128)(2,1)} %param.16) | copy-start | bytes 147460
  75.8 115.9 %copy-start.16 = (f32[256]{0:T(256)S(1)}, f32[256]{0:T(256)}, u32[]{:S(2)}) copy-start(f32[256]{0:T(256)} %param.24) | copy-start | bytes 3076
  77.2 225.1 %all-gather.8.cloned.1.call-start = ((), (), s32[]{:S(2)}) async-start(), calls=%async_computation.2 | async-start | bytes 2506752 | tf_op jit(solution)/shard_map/all_gather | solution.py:216
  192.6 7.5 %collective-permute-start.4 = (bf16[96,256]{1,0:T(8,128)(2,1)S(1)}, bf16[96,256]{1,0:T(8,128)(2,1)S(1)}, u32[]{:S(2)}, u32[]{:S(2)}) collective-permute-start(bf16[96,256]{1,0:T(8,128)(2,1)S(1)} %get-tuple-element.211), channel_id=1, source_target_pairs={{0,1},{1,2},{2,3},{3,4},{4,5},{5,6},{6,7},{7,8},{8,9},{9,10},{10,1... | collective-permute-start | bytes 147464 | tf_op jit(solution)/shard_map/ppermute | solution.py:190
  192.7 7.4 %collective-permute-start.5 = (bf16[96,256]{1,0:T(8,128)(2,1)S(1)}, bf16[96,256]{1,0:T(8,128)(2,1)S(1)}, u32[]{:S(2)}, u32[]{:S(2)}) collective-permute-start(bf16[96,256]{1,0:T(8,128)(2,1)S(1)} %get-tuple-element.211), channel_id=1, source_target_pairs={{0,15},{1,0},{2,1},{3,2},{4,3},{5,4},{6,5},{7,6},{8,7},{9,8},{10,9... | collective-permute-start | bytes 147464 | tf_op jit(solution)/shard_map/ppermute | solution.py:198
  200.1 7.4 %collective-permute-start.6 = (bf16[96,256]{1,0:T(8,128)(2,1)S(1)}, bf16[96,256]{1,0:T(8,128)(2,1)S(1)}, u32[]{:S(2)}, u32[]{:S(2)}) collective-permute-start(bf16[96,256]{1,0:T(8,128)(2,1)S(1)} %collective-permute-done.4), channel_id=1, source_target_pairs={{0,1},{1,2},{2,3},{3,4},{4,5},{5,6},{6,7},{7,8},{8,9},{9,10},{10,1... | collective-permute-start | bytes 147464 | tf_op jit(solution)/shard_map/ppermute | solution.py:190
  200.1 7.4 %collective-permute-start.7 = (bf16[96,256]{1,0:T(8,128)(2,1)S(1)}, bf16[96,256]{1,0:T(8,128)(2,1)S(1)}, u32[]{:S(2)}, u32[]{:S(2)}) collective-permute-start(bf16[96,256]{1,0:T(8,128)(2,1)S(1)} %collective-permute-done.5), channel_id=1, source_target_pairs={{0,15},{1,0},{2,1},{3,2},{4,3},{5,4},{6,5},{7,6},{8,7},{9,8},{10,9... | collective-permute-start | bytes 147464 | tf_op jit(solution)/shard_map/ppermute | solution.py:198
  207.5 7.7 %collective-permute-start.8 = (bf16[96,256]{1,0:T(8,128)(2,1)S(1)}, bf16[96,256]{1,0:T(8,128)(2,1)S(1)}, u32[]{:S(2)}, u32[]{:S(2)}) collective-permute-start(bf16[96,256]{1,0:T(8,128)(2,1)S(1)} %collective-permute-done.6), channel_id=1, source_target_pairs={{0,1},{1,2},{2,3},{3,4},{4,5},{5,6},{6,7},{7,8},{8,9},{9,10},{10,1... | collective-permute-start | bytes 147464 | tf_op jit(solution)/shard_map/ppermute | solution.py:190
  207.5 7.7 %collective-permute-start.9 = (bf16[96,256]{1,0:T(8,128)(2,1)S(1)}, bf16[96,256]{1,0:T(8,128)(2,1)S(1)}, u32[]{:S(2)}, u32[]{:S(2)}) collective-permute-start(bf16[96,256]{1,0:T(8,128)(2,1)S(1)} %collective-permute-done.7), channel_id=1, source_target_pairs={{0,15},{1,0},{2,1},{3,2},{4,3},{5,4},{6,5},{7,6},{8,7},{9,8},{10,9... | collective-permute-start | bytes 147464 | tf_op jit(solution)/shard_map/ppermute | solution.py:198
  215.1 7.4 %collective-permute-start.10 = (bf16[96,256]{1,0:T(8,128)(2,1)S(1)}, bf16[96,256]{1,0:T(8,128)(2,1)S(1)}, u32[]{:S(2)}, u32[]{:S(2)}) collective-permute-start(bf16[96,256]{1,0:T(8,128)(2,1)S(1)} %collective-permute-done.8), channel_id=1, source_target_pairs={{0,1},{1,2},{2,3},{3,4},{4,5},{5,6},{6,7},{7,8},{8,9},{9,10},{10,1... | collective-permute-start | bytes 147464 | tf_op jit(solution)/shard_map/ppermute | solution.py:190
  215.2 7.4 %collective-permute-start.11 = (bf16[96,256]{1,0:T(8,128)(2,1)S(1)}, bf16[96,256]{1,0:T(8,128)(2,1)S(1)}, u32[]{:S(2)}, u32[]{:S(2)}) collective-permute-start(bf16[96,256]{1,0:T(8,128)(2,1)S(1)} %collective-permute-done.9), channel_id=1, source_target_pairs={{0,15},{1,0},{2,1},{3,2},{4,3},{5,4},{6,5},{7,6},{8,7},{9,8},{10,9... | collective-permute-start | bytes 147464 | tf_op jit(solution)/shard_map/ppermute | solution.py:198
  222.6 7.4 %collective-permute-start.12 = (bf16[96,256]{1,0:T(8,128)(2,1)S(1)}, bf16[96,256]{1,0:T(8,128)(2,1)S(1)}, u32[]{:S(2)}, u32[]{:S(2)}) collective-permute-start(bf16[96,256]{1,0:T(8,128)(2,1)S(1)} %collective-permute-done.10), channel_id=1, source_target_pairs={{0,1},{1,2},{2,3},{3,4},{4,5},{5,6},{6,7},{7,8},{8,9},{9,10},{10,1... | collective-permute-start | bytes 147464 | tf_op jit(solution)/shard_map/ppermute | solution.py:190
  222.6 7.4 %collective-permute-start.13 = (bf16[96,256]{1,0:T(8,128)(2,1)S(1)}, bf16[96,256]{1,0:T(8,128)(2,1)S(1)}, u32[]{:S(2)}, u32[]{:S(2)}) collective-permute-start(bf16[96,256]{1,0:T(8,128)(2,1)S(1)} %collective-permute-done.11), channel_id=1, source_target_pairs={{0,15},{1,0},{2,1},{3,2},{4,3},{5,4},{6,5},{7,6},{8,7},{9,8},{10,9... | collective-permute-start | bytes 147464 | tf_op jit(solution)/shard_map/ppermute | solution.py:198
  230.0 7.4 %collective-permute-start.14 = (bf16[96,256]{1,0:T(8,128)(2,1)S(1)}, bf16[96,256]{1,0:T(8,128)(2,1)S(1)}, u32[]{:S(2)}, u32[]{:S(2)}) collective-permute-start(bf16[96,256]{1,0:T(8,128)(2,1)S(1)} %collective-permute-done.12), channel_id=1, source_target_pairs={{0,1},{1,2},{2,3},{3,4},{4,5},{5,6},{6,7},{7,8},{8,9},{9,10},{10,1... | collective-permute-start | bytes 147464 | tf_op jit(solution)/shard_map/ppermute | solution.py:190
  230.0 7.4 %collective-permute-start.15 = (bf16[96,256]{1,0:T(8,128)(2,1)S(1)}, bf16[96,256]{1,0:T(8,128)(2,1)S(1)}, u32[]{:S(2)}, u32[]{:S(2)}) collective-permute-start(bf16[96,256]{1,0:T(8,128)(2,1)S(1)} %collective-permute-done.13), channel_id=1, source_target_pairs={{0,15},{1,0},{2,1},{3,2},{4,3},{5,4},{6,5},{7,6},{8,7},{9,8},{10,9... | collective-permute-start | bytes 147464 | tf_op jit(solution)/shard_map/ppermute | solution.py:198
  237.4 7.4 %collective-permute-start.16 = (bf16[96,256]{1,0:T(8,128)(2,1)S(1)}, bf16[96,256]{1,0:T(8,128)(2,1)S(1)}, u32[]{:S(2)}, u32[]{:S(2)}) collective-permute-start(bf16[96,256]{1,0:T(8,128)(2,1)S(1)} %collective-permute-done.14), channel_id=1, source_target_pairs={{0,1},{1,2},{2,3},{3,4},{4,5},{5,6},{6,7},{7,8},{8,9},{9,10},{10,1... | collective-permute-start | bytes 147464 | tf_op jit(solution)/shard_map/ppermute | solution.py:190
  237.4 7.4 %collective-permute-start.17 = (bf16[96,256]{1,0:T(8,128)(2,1)S(1)}, bf16[96,256]{1,0:T(8,128)(2,1)S(1)}, u32[]{:S(2)}, u32[]{:S(2)}) collective-permute-start(bf16[96,256]{1,0:T(8,128)(2,1)S(1)} %collective-permute-done.15), channel_id=1, source_target_pairs={{0,15},{1,0},{2,1},{3,2},{4,3},{5,4},{6,5},{7,6},{8,7},{9,8},{10,9... | collective-permute-start | bytes 147464 | tf_op jit(solution)/shard_map/ppermute | solution.py:198
  244.8 7.4 %collective-permute-start.18 = (bf16[96,256]{1,0:T(8,128)(2,1)S(1)}, bf16[96,256]{1,0:T(8,128)(2,1)S(1)}, u32[]{:S(2)}, u32[]{:S(2)}) collective-permute-start(bf16[96,256]{1,0:T(8,128)(2,1)S(1)} %collective-permute-done.16), channel_id=1, source_target_pairs={{0,1},{1,2},{2,3},{3,4},{4,5},{5,6},{6,7},{7,8},{8,9},{9,10},{10,1... | collective-permute-start | bytes 147464 | tf_op jit(solution)/shard_map/ppermute | solution.py:190
  252.2 4.7 %copy-start.17 = (s32[2,4]{1,0:T(2,128)S(1)}, s32[2,4]{1,0:T(2,128)}, u32[]{:S(2)}) copy-start(s32[2,4]{1,0:T(2,128)} %param.22) | copy-start | bytes 100
  252.2 5.0 %slice-start = ((bf16[3,96,256]{2,1,0:T(8,128)(2,1)}), bf16[2,96,256]{2,1,0:T(8,128)(2,1)S(1)}, s32[]{:S(2)}) async-start(bf16[3,96,256]{2,1,0:T(8,128)(2,1)} %param.17), calls=%async_computation.3 | async-start | bytes 196608 | tf_op jit(solution)/shard_map/slice | solution.py:230
  311.4 0.7 copy-start.15
Sparse Core Ops, SparseCore 0:
  77.3 75.2 reduce-scatter.1
  257.0 45.2 all-gather.7
